TPU v7x, 512 devices: a whole 4x4x16 slice. The times are simulated.
512 devices in a mesh: group: 8 (over x, z_hi), rollout: 64 (over y, z_lo, core).
Axes of the slice: x: 4, y: 4, z: 16 (z_hi: 2, z_lo: 8; z = z_hi * 8 + z_lo), core: 2. Of those that a mesh axis runs over, the one named last changes fastest.
Arguments:
- queries: bfloat16 [65536, 2048], P(('group', 'rollout')), parts along dimension 0, may hold values from -120 to 120
- roll_kv: bfloat16 [2, 65536, 512], P(None, ('group', 'rollout')), parts along dimension 1, may hold values from -6 to 6
- prefix_kv: bfloat16 [4096, 2, 512], P(('group', 'rollout')), parts along dimension 0, may hold values from -6.2 to 6.2
- grad_seed: bfloat16 [65536, 2048], P(('group', 'rollout')), parts along dimension 0, may hold values from -6 to 6
- lengths: int32 [512], P(('group', 'rollout')), parts along dimension 0, may hold values from 1 to 128, 6144 in all
- rewards: int32 [512], P(('group', 'rollout')), parts along dimension 0, may hold values from 10 to 70
Outputs:
- grad_queries: bfloat16 [65536, 2048], P(('group', 'rollout')), parts along dimension 0
- grad_roll_kv: bfloat16 [2, 65536, 512], P(None, ('group', 'rollout')), parts along dimension 1
- grad_prefix_kv: bfloat16 [4096, 2, 512], P(('group', 'rollout')), parts along dimension 0
There are 8 independent parts, one for each index of `group`. A program takes and returns all parts, laid end to end along the dimension named above; each array names one. Nothing has to cross between parts.
All inputs are finite; a program needn't handle non-finite values. No bound on the sum of `lengths` on one device may be relied on, other than what follows from the above.
Results may differ from a plain program's by a relative error of at most 0.0095.
Values may be sent and summed in bfloat16 or wider, within the bound.
A program may use at most 64 MiB of HBM per device.

v0:
```python
import math

import jax
import jax.numpy as jnp
from jax import lax
from jax.sharding import PartitionSpec as P

HQ = 16
HK = 4
HD = 128


score_floor = -1e30


def head_scores(query_head, key_head, score_scale):
    return (
        jnp.einsum("tgd,nd->gtn", query_head, key_head, preferred_element_type=jnp.float32)
        * score_scale
    )


def local(queries, roll_kv, prefix_kv, grad_seed, lengths, rewards):
    row_count = queries.shape[0]
    group_size = HQ // HK
    score_scale = 1.0 / math.sqrt(HD)
    rollout_count = lax.axis_size("rollout")
    reward_vals = rewards.astype(jnp.float32)
    totals = lax.psum(
        (
            jnp.sum(reward_vals),
            jnp.sum(reward_vals * reward_vals),
            jnp.sum(lengths.astype(jnp.float32)),
        ),
        "rollout",
    )
    reward_mean = totals[0] / rollout_count
    reward_var = totals[1] / rollout_count - reward_mean * reward_mean
    reward_std = jnp.sqrt(reward_var)
    token_weight = (
        (reward_vals[0] - reward_mean)
        / (reward_std + 1.0)
        * (float(rollout_count * row_count) / totals[2])
    )
    position = jnp.arange(row_count, dtype=jnp.int32)
    live_row = position < lengths[0]
    grad_bf = jnp.where(
        live_row[:, None], token_weight * grad_seed.astype(jnp.float32), 0.0
    ).astype(jnp.bfloat16)
    prefix_all = lax.all_gather(prefix_kv, "rollout", axis=0, tiled=True)
    prefix_rows = prefix_all.shape[0]
    all_keys = jnp.concatenate([prefix_all[:, 0], roll_kv[0]], axis=0)
    all_values = jnp.concatenate([prefix_all[:, 1], roll_kv[1]], axis=0)
    column = jnp.arange(prefix_rows + row_count, dtype=jnp.int32)
    allowed = (column[None, :] < prefix_rows) | (column[None, :] - prefix_rows <= position[:, None])
    query_heads = queries.reshape(row_count, HK, group_size, HD)
    grad_heads = grad_bf.reshape(row_count, HK, group_size, HD)
    first_key = 0
    query_parts, key_grads, value_grads, log_parts, dot_parts = ([], [], [], [], [])
    for kv_head in range(HK):
        query_head = query_heads[:, kv_head]
        grad_head = grad_heads[:, kv_head]
        key_head = all_keys[:, kv_head * HD : (kv_head + 1) * HD]
        value_head = all_values[:, kv_head * HD : (kv_head + 1) * HD]
        scores = jnp.where(
            allowed[None], head_scores(query_head, key_head, score_scale), score_floor
        )
        row_max = jnp.max(scores, axis=-1, keepdims=True)
        log_total = row_max + jnp.log(jnp.sum(jnp.exp(scores - row_max), axis=-1, keepdims=True))
        softmax = jnp.exp(scores - log_total)
        soft_bf = softmax.astype(jnp.bfloat16)
        attended = jnp.einsum(
            "gtn,nd->gtd", soft_bf, value_head, preferred_element_type=jnp.float32
        )
        row_dot = jnp.einsum("tgd,gtd->gt", grad_head.astype(jnp.float32), attended)[..., None]
        grad_soft = jnp.einsum(
            "tgd,nd->gtn", grad_head, value_head, preferred_element_type=jnp.float32
        )
        score_bf = (softmax * (grad_soft - row_dot)).astype(jnp.bfloat16)
        query_parts.append(
            jnp.einsum("gtn,nd->tgd", score_bf, key_head, preferred_element_type=jnp.float32)
            * score_scale
        )
        key_grads.append(
            jnp.einsum("gtn,tgd->nd", score_bf, query_head, preferred_element_type=jnp.float32)
            * score_scale
        )
        value_grads.append(
            jnp.einsum("gtn,tgd->nd", soft_bf, grad_head, preferred_element_type=jnp.float32)
        )
        log_parts.append(log_total)
        dot_parts.append(row_dot)
    grad_query = jnp.stack(query_parts, axis=1).reshape(row_count, HQ * HD).astype(jnp.bfloat16)
    grad_key = jnp.concatenate(key_grads, axis=1)
    grad_value = jnp.concatenate(value_grads, axis=1)
    own_grads = jnp.stack([grad_key[-row_count:], grad_value[-row_count:]], axis=0).astype(
        jnp.bfloat16
    )
    prefix_term = jnp.stack([grad_key[:prefix_rows], grad_value[:prefix_rows]], axis=1)
    prefix_sum = lax.psum_scatter(prefix_term, "rollout", scatter_dimension=0, tiled=True)
    return (grad_query, own_grads, prefix_sum.astype(jnp.bfloat16))


def solution(mesh):
    return jax.shard_map(
        local,
        mesh=mesh,
        in_specs=(
            P(("group", "rollout"), None),
            P(None, ("group", "rollout"), None),
            P(("group", "rollout"), None, None),
            P(("group", "rollout"), None),
            P(("group", "rollout")),
            P(("group", "rollout")),
        ),
        out_specs=(
            P(("group", "rollout"), None),
            P(None, ("group", "rollout"), None),
            P(("group", "rollout"), None, None),
        ),
        check_vma=False,
    )
```

profile of v0, /device:TPU:1, one launch (start us, length us, event | category | flops | bytes accessed | tf_op | source)
XLA Modules:
  0.0 702.1 jit_solution(13675991732635555908)
XLA Ops:
  7.2 1.4 copy.75
  9.9 219.1 %all-reduce.1 = (f32[]{:T(128)}, f32[]{:T(128)}, f32[]{:T(128)}) all-reduce(f32[]{:T(128)} %bitcast.15, f32[]{:T(128)} %bitcast.16, f32[]{:T(128)} %bitcast.17), channel_id=1, replica_groups=mesh['group'=8,'rollout'=64] {'rollout'}, use_global_device_ids=true, to_apply=%region_2.0 | all-reduce | flops 3 | bytes 24 | tf_op jit(solution)/shard_map/psum | solution.py:29
  231.6 1.3 copy.76
  234.7 1.3 dynamic-slice
  237.0 1.3 slice_bitcast_fusion.2
  238.2 0.3 fusion.107
  238.8 0.4 convolution_bitcast_fusion.5
  239.2 0.5 fusion.34
  239.7 0.4 fusion.18
  240.3 0.3 fusion.21
  240.7 0.3 fusion.108
  241.2 0.4 convolution_bitcast_fusion.6
  241.6 0.5 fusion.33
  242.1 0.4 fusion.17
  242.7 0.3 fusion.22
  243.1 0.3 fusion.109
  243.6 0.4 convolution_bitcast_fusion.7
  244.0 0.5 fusion.32
  244.5 0.4 fusion.16
  245.2 0.3 fusion.23
  245.5 0.3 fusion.106
  246.1 0.4 convolution_bitcast_fusion.4
  246.4 0.5 fusion.35
  246.9 0.4 fusion.19
  247.3 0.3 fusion.20
  248.3 1.1 slice_bitcast_fusion.1
  249.5 1.0 copy.115
  250.5 1.4 pad_maximum_fusion
  251.9 2.5 copy.114
  254.4 439.4 %all-reduce.3 = bf16[512,2,512]{2,1,0:T(2,128)(2,1)S(1)} all-reduce(f32[512,2,512]{2,1,0:T(2,128)} %copy.114), channel_id=2, replica_groups=mesh['group'=8,'rollout'=64] {'rollout'}, use_global_device_ids=true, to_apply=%region_11.12.clone | all-reduce | flops 524288 | bytes 3145728
  693.8 0.9 copy.116
  694.6 0.6 dynamic-slice_convert_fusion
  (39 shorter events, 3.8 us)
Async XLA Ops:
  7.2 225.7 %copy-start = (bf16[128,2048]{1,0:T(8,128)(2,1)S(1)}, bf16[128,2048]{1,0:T(8,128)(2,1)}, u32[]{:S(2)}) copy-start(bf16[128,2048]{1,0:T(8,128)(2,1)} %param.9) | copy-start | bytes 1572868
  7.2 229.8 %all-gather.2.cloned.1.call-start = ((), (), s32[]{:S(2)}) async-start(), calls=%async_computation | async-start | bytes 1064960 | tf_op jit(solution)/shard_map/all_gather | solution.py:50
  234.1 2.8 copy-start.1
Sparse Core Ops, SparseCore 0:
  10.7 125.0 all-gather.1
where the time goes:
time: 712 us; the launch traced here: 702 us
  blocking collectives  658 us (92%)
  between operations  19.7 us (3%)
  local copies, waits for them, and re-layouts  12.3 us (2%)
  matrix products  8.66 us (1%)
    unnamed x1, blocking collectives  439 us
    psum x1, blocking collectives, local(): lax.psum((jnp.sum(reward_vals), jnp.sum(reward_vals * reward_vals), jnp.s...  219 us
  transfers between devices with their start and end apart: 1, of which 0 were waited for; matrix products, arithmetic and copies ran while one was open for 1% of the time, Pallas kernels for 0%

commit v1 on v0

v1 whole, which is shorter than its diff:
```python
import functools
import math

import jax
import jax.numpy as jnp
from jax import lax
from jax.experimental import pallas as pl
from jax.experimental.pallas import tpu as pltpu
from jax.sharding import PartitionSpec as P

HD = 128
GROUP = 4
NY = 4
NZ = 8
ROWS = 128
SCALE = 1.0 / math.sqrt(HD)
LOG2E = 1.4426950408889634
MESH = pl.DeviceIdType.MESH
F32 = jnp.float32
BF16 = jnp.bfloat16
NT = (((1,), (1,)), ((), ()))
TN = (((0,), (0,)), ((), ()))


def dot(a, b, dims=(((1,), (0,)), ((), ()))):
    return lax.dot_general(a, b, dims, preferred_element_type=F32)


def kernel(
    q_hbm, rkv_hbm, pkv_ref, do_hbm, len_ref, rew_ref,
    gq_hbm, grkv_hbm, gp_ref,
    kvblk, zrecv, kv_all, stat_own, statz, staty_own, staty,
    q_in, do_in, rkv_in, qcat, docat, p_sc, ds_sc,
    ysend, yrecv, yown, zsend, zback, gq_st, grkv_st,
    zs_sem, zr_sem, ss_sem, sr_sem, ys_sem, yr_sem, sys_sem, syr_sem,
    in_sem, xs_sem, xr_sem, rys_sem, ryr_sem, rzs_sem, rzr_sem, out_sem, os_sem, or_sem,
):
    group = lax.axis_index("group")
    index = lax.axis_index("rollout")
    y = index // (2 * NZ)
    z = (index // 2) % NZ
    core = index % 2
    other = 1 - core
    prefix = NY * NZ * 16

    def device(yy, zz, cc):
        return (group, (yy * NZ + zz) * 2 + cc)

    def remote(src, dst, ssem, rsem, where):
        return pltpu.make_async_remote_copy(
            src_ref=src, dst_ref=dst, send_sem=ssem, recv_sem=rsem,
            device_id=where, device_id_type=MESH,
        )

    column = [(d, e) for d in range(NZ) for e in range(2) if d or e]

    def peer(d, e):
        return device(y, z ^ d, core ^ e)

    barrier = pltpu.get_barrier_semaphore()
    for d, e in column:
        pl.semaphore_signal(barrier, inc=1, device_id=peer(d, e), device_id_type=MESH)
    for d in range(1, NY):
        pl.semaphore_signal(
            barrier, inc=1, device_id=device((y + d) % NY, z, core), device_id_type=MESH
        )

    my_q = pl.multiple_of(core * 1024, 1024)
    other_q = pl.multiple_of(other * 1024, 1024)
    my_kv = pl.multiple_of(core * 256, 256)
    other_kv = pl.multiple_of(other * 256, 256)
    loads = [
        pltpu.make_async_copy(q_hbm.at[:, pl.ds(my_q, 1024)], q_in.at[core], in_sem.at[0]),
        pltpu.make_async_copy(do_hbm.at[:, pl.ds(my_q, 1024)], do_in.at[core], in_sem.at[1]),
        pltpu.make_async_copy(rkv_hbm.at[:, :, pl.ds(my_kv, 256)], rkv_in.at[core], in_sem.at[2]),
    ]
    for load in loads:
        load.start()

    pair = pkv_ref[...].astype(F32)
    own_k = pair[:, 0, :]
    own_v = pair[:, 1, :]
    for cc in range(2):
        cols = slice(cc * 256, cc * 256 + 256)
        kvblk[cc] = jnp.concatenate([own_k[:, cols], own_v[:, cols]], axis=0).astype(BF16)
    zrecv[z * 2 + core] = kvblk[core]

    lane = lax.broadcasted_iota(jnp.int32, (1, 128), 1)
    reward = rew_ref[0].astype(F32)
    length = len_ref[0].astype(F32)
    stat = jnp.where(
        lane == 0, reward, jnp.where(lane == 1, reward * reward, jnp.where(lane == 2, length, 0.0))
    )
    stat_own[0] = stat
    statz[z * 2 + core] = stat

    pl.semaphore_wait(barrier, len(column) + NY - 1)

    zcopies = []
    for i, (d, e) in enumerate(column):
        zcopies.append(
            remote(
                kvblk.at[core ^ e], zrecv.at[z * 2 + core], zs_sem.at[i],
                zr_sem.at[d * 2 + e], peer(d, e),
            )
        )
        zcopies[-1].start()
    scopies = []
    for i, (d, e) in enumerate(column):
        scopies.append(
            remote(
                stat_own.at[0], statz.at[z * 2 + core], ss_sem.at[i], sr_sem.at[d * 2 + e], peer(d, e)
            )
        )
        scopies[-1].start()
    partner = device(y, z, other)
    xcopies = [
        remote(q_hbm.at[:, pl.ds(other_q, 1024)], q_in.at[core], xs_sem.at[0], xr_sem.at[0], partner),
        remote(do_hbm.at[:, pl.ds(other_q, 1024)], do_in.at[core], xs_sem.at[1], xr_sem.at[1], partner),
        remote(
            rkv_hbm.at[:, :, pl.ds(other_kv, 256)], rkv_in.at[core], xs_sem.at[2], xr_sem.at[2], partner
        ),
    ]
    for copy in xcopies:
        copy.start()

    ycopies = []
    for d in range(NZ):
        for e in range(2):
            if d or e:
                slot = (z ^ d) * 2 + (core ^ e)
                remote(
                    kvblk.at[0], zrecv.at[slot], zs_sem.at[0], zr_sem.at[d * 2 + e], peer(d, e)
                ).wait_recv()
        zz = z ^ d
        first = zrecv[zz * 2].astype(F32)
        second = zrecv[zz * 2 + 1].astype(F32)
        at = pl.ds(pl.multiple_of(y * (NZ * 16) + zz * 16, 16), 16)
        kv_all[0, at, :] = jnp.concatenate([first[:8], second[:8]], axis=0).astype(BF16)
        kv_all[1, at, :] = jnp.concatenate([first[8:], second[8:]], axis=0).astype(BF16)
        for k in range(1, NY):
            copy = remote(
                kv_all.at[:, at, :], kv_all.at[:, at, :], ys_sem.at[d * (NY - 1) + k - 1],
                yr_sem.at[k - 1], device((y + k) % NY, z, core),
            )
            copy.start()
            ycopies.append(copy)

    for i, (d, e) in enumerate(column):
        slot = (z ^ d) * 2 + (core ^ e)
        remote(
            stat_own.at[0], statz.at[slot], ss_sem.at[0], sr_sem.at[d * 2 + e], peer(d, e)
        ).wait_recv()
    column_sum = jnp.sum(statz[...], axis=0)
    staty_own[0] = column_sum
    staty[y] = column_sum
    sycopies = []
    for k in range(1, NY):
        copy = remote(
            staty_own.at[0], staty.at[y], sys_sem.at[k - 1], syr_sem.at[k - 1],
            device((y + k) % NY, z, core),
        )
        copy.start()
        sycopies.append(copy)

    for load in loads:
        load.wait()
    for copy in xcopies:
        copy.wait_recv()

    for hd in range(2):
        for j in range(2):
            for g in range(GROUP):
                col = hd * 512 + g * HD
                qcat[hd, 2 * j + g // 2, (g % 2) * ROWS : (g % 2 + 1) * ROWS, :] = q_in[
                    j, :, col : col + HD
                ]

    for k in range(1, NY):
        yy = (y + NY - k) % NY
        remote(
            staty_own.at[0], staty.at[yy], sys_sem.at[0], syr_sem.at[k - 1], device(yy, z, core)
        ).wait_recv()
    totals = jnp.sum(staty[...], axis=0)
    rollouts = float(2 * NY * NZ)
    mean = totals[:, 0:1] / rollouts
    var = totals[:, 1:2] / rollouts - mean * mean
    divisor = jnp.sqrt(var) + 1.0
    norm = float(2 * NY * NZ * ROWS) / totals[:, 2:3]
    row = lax.broadcasted_iota(jnp.int32, (ROWS, HD), 0).astype(F32)
    for j in range(2):
        own = statz[z * 2 + j]
        weight = (own[:, 0:1] - mean) / divisor * norm
        live = row < own[:, 2:3]
        for hd in range(2):
            for g in range(GROUP):
                col = hd * 512 + g * HD
                seed = do_in[j, :, col : col + HD].astype(F32)
                docat[hd, 2 * j + g // 2, (g % 2) * ROWS : (g % 2 + 1) * ROWS, :] = jnp.where(
                    live, weight * seed, 0.0
                ).astype(BF16)

    for k in range(1, NY):
        yy = (y + NY - k) % NY
        at = pl.ds(pl.multiple_of(yy * (NZ * 16), NZ * 16), NZ * 16)
        remote(
            kv_all.at[:, at, :], kv_all.at[:, at, :], ys_sem.at[0], yr_sem.at[k - 1], device(yy, z, core)
        ).wait_recv()

    def strips(hd):
        cols = slice(hd * HD, (hd + 1) * HD)

        def strip(s, carry):
            j = s // 2
            q = qcat[hd, s]
            do = docat[hd, s]
            kp = kv_all[0, :, cols]
            vp = kv_all[1, :, cols]
            ko = rkv_in[j, 0, :, cols]
            vo = rkv_in[j, 1, :, cols]
            key = lax.broadcasted_iota(jnp.int32, (ROWS, 256), 0)
            query = lax.broadcasted_iota(jnp.int32, (ROWS, 256), 1) % ROWS
            sp = dot(kp, q, NT)
            so = jnp.where(key <= query, dot(ko, q, NT), -1e30)
            top = jnp.maximum(
                jnp.max(sp, axis=0, keepdims=True), jnp.max(so, axis=0, keepdims=True)
            )
            ep = jnp.exp2((sp - top) * (SCALE * LOG2E))
            eo = jnp.exp2((so - top) * (SCALE * LOG2E))
            total = jnp.sum(ep, axis=0, keepdims=True) + jnp.sum(eo, axis=0, keepdims=True)
            inverse = 1.0 / total
            dp = dot(vp, do, NT)
            dn = dot(vo, do, NT)
            row_dot = (
                jnp.sum(ep * dp, axis=0, keepdims=True) + jnp.sum(eo * dn, axis=0, keepdims=True)
            ) * inverse
            pp = ep * inverse
            po = eo * inverse
            at = pl.ds(pl.multiple_of(s * 256, 256), 256)
            p_sc[:prefix, at] = pp.astype(BF16)
            p_sc[prefix:, at] = po.astype(BF16)
            ds_sc[:prefix, at] = (pp * (dp - row_dot)).astype(BF16)
            ds_sc[prefix:, at] = (po * (dn - row_dot)).astype(BF16)
            return carry

        lax.fori_loop(0, 4, strip, 0)

    rycopies = []

    def prefix_grads(hd):
        qs = qcat[hd].reshape(1024, HD)
        dos = docat[hd].reshape(1024, HD)
        for k in range(1, NY + 1):
            yy = (y + k) % NY
            at = pl.ds(pl.multiple_of(yy * (NZ * 16), NZ * 16), NZ * 16)
            gk = dot(ds_sc[at, :], qs) * SCALE
            gv = dot(p_sc[at, :], dos)
            if k == NY:
                yown[hd, 0] = gk
                yown[hd, 1] = gv
            else:
                ysend[hd, k - 1, 0] = gk.astype(BF16)
                ysend[hd, k - 1, 1] = gv.astype(BF16)
                copy = remote(
                    ysend.at[hd, k - 1], yrecv.at[hd, k - 1], rys_sem.at[hd, k - 1],
                    ryr_sem.at[hd, k - 1], device(yy, z, core),
                )
                copy.start()
                rycopies.append(copy)

    def local_grads(hd):
        cols = slice(hd * HD, (hd + 1) * HD)
        for j in range(2):
            qs = qcat[hd, 2 * j : 2 * j + 2].reshape(512, HD)
            dos = docat[hd, 2 * j : 2 * j + 2].reshape(512, HD)
            at = slice(j * 512, j * 512 + 512)
            grkv_st[j, 0, :, cols] = (dot(ds_sc[prefix:, at], qs) * SCALE).astype(BF16)
            grkv_st[j, 1, :, cols] = dot(p_sc[prefix:, at], dos).astype(BF16)

        def query_strip(s, carry):
            j = s // 2
            at = pl.ds(pl.multiple_of(s * 256, 256), 256)
            kp = kv_all[0, :, cols]
            ko = rkv_in[j, 0, :, cols]
            grad = dot(kp, ds_sc[:prefix, at], TN) + dot(ko, ds_sc[prefix:, at], TN)
            grad = (grad * SCALE).T.astype(BF16)
            for g in range(2):
                col = pl.multiple_of(hd * 512 + (s % 2) * 256 + g * HD, HD)
                gq_st[j, :, pl.ds(col, HD)] = grad[g * ROWS : (g + 1) * ROWS]
            return carry

        lax.fori_loop(0, 4, query_strip, 0)

    rzcopies = []

    def row_sums(hd):
        for k in range(1, NY):
            remote(
                ysend.at[hd, k - 1], yrecv.at[hd, k - 1], rys_sem.at[hd, k - 1],
                ryr_sem.at[hd, k - 1], device((y + NY - k) % NY, z, core),
            ).wait_recv()
        sums = [
            yown[hd, i]
            + (yrecv[hd, 0, i].astype(F32) + yrecv[hd, 1, i].astype(F32) + yrecv[hd, 2, i].astype(F32))
            for i in range(2)
        ]
        for zz in range(NZ):
            for cc in range(2):
                at = slice(zz * 16 + cc * 8, zz * 16 + cc * 8 + 8)
                zsend[hd, zz * 2 + cc] = jnp.concatenate([sums[0][at], sums[1][at]], axis=0).astype(BF16)
        zback[hd, z * 2 + core] = zsend[hd, z * 2 + core]
        for i, (d, e) in enumerate(column):
            copy = remote(
                zsend.at[hd, (z ^ d) * 2 + (core ^ e)], zback.at[hd, z * 2 + core],
                rzs_sem.at[hd, i], rzr_sem.at[hd, d * 2 + e], peer(d, e),
            )
            copy.start()
            rzcopies.append(copy)

    strips(0)
    prefix_grads(0)
    local_grads(0)
    strips(1)
    prefix_grads(1)
    row_sums(0)
    local_grads(1)
    outs = [
        pltpu.make_async_copy(gq_st.at[core], gq_hbm.at[:, pl.ds(my_q, 1024)], out_sem.at[0]),
        pltpu.make_async_copy(grkv_st.at[core], grkv_hbm.at[:, :, pl.ds(my_kv, 256)], out_sem.at[1]),
    ]
    ocopies = [
        remote(gq_st.at[other], gq_hbm.at[:, pl.ds(my_q, 1024)], os_sem.at[0], or_sem.at[0], partner),
        remote(
            grkv_st.at[other], grkv_hbm.at[:, :, pl.ds(my_kv, 256)], os_sem.at[1], or_sem.at[1], partner
        ),
    ]
    for copy in ocopies + outs:
        copy.start()
    row_sums(1)

    for hd in range(2):
        for d, e in column:
            slot = (z ^ d) * 2 + (core ^ e)
            remote(
                zsend.at[hd, slot], zback.at[hd, slot], rzs_sem.at[hd, 0],
                rzr_sem.at[hd, d * 2 + e], peer(d, e),
            ).wait_recv()
    for cc in range(2):
        for hd in range(2):
            total = zback[hd, cc].astype(F32)
            for zz in range(1, NZ):
                total = total + zback[hd, zz * 2 + cc].astype(F32)
            cols = slice(cc * 256 + hd * HD, cc * 256 + (hd + 1) * HD)
            gp_ref[0, :, cols] = total[:8]
            gp_ref[1, :, cols] = total[8:]

    for copy in outs:
        copy.wait()
    for copy in ocopies:
        copy.wait()
    for copy in zcopies + scopies + xcopies + ycopies + sycopies + rycopies + rzcopies:
        copy.wait_send()


def local(queries, roll_kv, prefix_kv, grad_seed, lengths, rewards):
    prefix = NY * NZ * 16
    keys = prefix + ROWS
    near = NZ * 16
    vmem = pltpu.VMEM
    sem = pltpu.SemaphoreType.DMA
    anywhere = pl.BlockSpec(memory_space=pl.ANY)
    whole = pl.BlockSpec(memory_space=pltpu.VMEM)
    scalar = pl.BlockSpec(memory_space=pltpu.SMEM)
    ncol = 2 * NZ
    gq, grkv, gp = pl.pallas_call(
        kernel,
        out_shape=(
            jax.ShapeDtypeStruct(queries.shape, BF16),
            jax.ShapeDtypeStruct(roll_kv.shape, BF16),
            jax.ShapeDtypeStruct((2, 8, 512), F32),
        ),
        in_specs=[anywhere, anywhere, whole, anywhere, scalar, scalar],
        out_specs=(anywhere, anywhere, whole),
        scratch_shapes=[
            vmem((2, 16, 256), BF16),
            vmem((ncol, 16, 256), BF16),
            vmem((2, prefix, 256), BF16),
            vmem((1, 1, 128), F32),
            vmem((ncol, 1, 128), F32),
            vmem((1, 1, 128), F32),
            vmem((NY, 1, 128), F32),
            vmem((2, ROWS, 1024), BF16),
            vmem((2, ROWS, 1024), BF16),
            vmem((2, 2, ROWS, 256), BF16),
            vmem((2, 4, 256, HD), BF16),
            vmem((2, 4, 256, HD), BF16),
            vmem((keys, 1024), BF16),
            vmem((keys, 1024), BF16),
            vmem((2, NY - 1, 2, near, HD), BF16),
            vmem((2, NY - 1, 2, near, HD), BF16),
            vmem((2, 2, near, HD), F32),
            vmem((2, ncol, 16, HD), BF16),
            vmem((2, ncol, 16, HD), BF16),
            vmem((2, ROWS, 1024), BF16),
            vmem((2, 2, ROWS, 256), BF16),
            sem((ncol,)), sem((ncol,)),
            sem((ncol,)), sem((ncol,)),
            sem((NZ * (NY - 1),)), sem((NY - 1,)),
            sem((NY - 1,)), sem((NY - 1,)),
            sem((3,)), sem((3,)), sem((3,)),
            sem((2, NY - 1)), sem((2, NY - 1)),
            sem((2, ncol)), sem((2, ncol)),
            sem((2,)), sem((2,)), sem((2,)),
        ],
        compiler_params=pltpu.CompilerParams(
            collective_id=0, has_side_effects=True, vmem_limit_bytes=40 * 2**20
        ),
        name="prefix_attention_backward",
    )(queries, roll_kv, prefix_kv, grad_seed, lengths, rewards)
    return gq, grkv, gp.transpose(1, 0, 2).astype(BF16)


def solution(mesh):
    rows = ("group", "rollout")
    return jax.shard_map(
        local,
        mesh=mesh,
        in_specs=(
            P(rows, None), P(None, rows, None), P(rows, None, None), P(rows, None), P(rows), P(rows),
        ),
        out_specs=(P(rows, None), P(None, rows, None), P(rows, None, None)),
        check_vma=False,
    )
```

time: 712 us -> 56.9 us (0.08); the launches traced: 702 us -> 56.6 us
  blocking collectives: 658 us -> 0 us
  Pallas kernels: 0 us -> 48.8 us
  between operations: 19.7 us -> 1.95 us
  matrix products: 8.66 us -> 0 us
    unnamed x1 -> x0, blocking collectives: 439 us -> none
    psum x1 -> x0, blocking collectives: 219 us -> none  [local(): lax.psum((jnp.sum(reward_vals), jnp.sum(reward_vals * reward_vals), jnp.s...]
    pallas_call x0 -> x1, Pallas kernels: none -> 48.8 us  [local(): pl.pallas_call(kernel, out_shape=(jax.ShapeDtypeStruct(queries.shape, BF1...]
    dot_general x24 -> x0, matrix products: 8.66 us -> none  [the longest x4 1.89 us: local(): jnp.einsum('gtn,nd->gtd', soft_bf, value_head, preferred_element_type=jnp...]
  transfers between devices with their start and end apart: 1 -> 0, of which waited for: 0 -> 0; matrix products, arithmetic and copies ran while one was open for 1% -> 0% of each run, Pallas kernels for 0% -> 0%
where the time goes in v1:
time: 56.9 us; the launch traced here: 56.6 us
  Pallas kernels  48.8 us (86%)
  local copies, waits for them, and re-layouts  5.86 us (10%)
  between operations  1.95 us (3%)
    pallas_call x1, Pallas kernels, local(): pl.pallas_call(kernel, out_shape=(jax.ShapeDtypeStruct(queries.shape, BF1...  48.8 us
    unnamed x11, local copies, waits for them, and re-layouts  5.86 us

profile of v1, /device:TPU:1, one launch (start us, length us, event | category | flops | bytes accessed | tf_op | source)
XLA Modules:
  0.0 56.6 jit_solution(1142303386360822502)
XLA Ops:
  1.9 0.0 copy-start
  1.9 1.0 %copy-done = bf16[128,2048]{1,0:T(8,128)(2,1)S(1)} copy-done((bf16[128,2048]{1,0:T(8,128)(2,1)S(1)}, bf16[128,2048]{1,0:T(8,128)(2,1)}, u32[]{:S(2)}) %copy-start) | copy-done | bytes 524312
  3.0 0.0 copy-start.1
  3.0 1.0 %copy-done.1 = bf16[128,2048]{1,0:T(8,128)(2,1)S(1)} copy-done((bf16[128,2048]{1,0:T(8,128)(2,1)S(1)}, bf16[128,2048]{1,0:T(8,128)(2,1)}, u32[]{:S(2)}) %copy-start.1) | copy-done | bytes 524312
  4.0 0.0 copy-start.2
  4.0 0.9 %copy-done.2 = bf16[2,128,512]{2,1,0:T(8,128)(2,1)S(1)} copy-done((bf16[2,128,512]{2,1,0:T(8,128)(2,1)S(1)}, bf16[2,128,512]{2,1,0:T(8,128)(2,1)}, u32[]{:S(2)}) %copy-start.2) | copy-done | bytes 262168
  5.0 0.0 copy-start.3
  5.0 0.7 %copy-done.3 = bf16[8,2,512]{2,1,0:T(2,128)(2,1)S(1)} copy-done((bf16[8,2,512]{2,1,0:T(2,128)(2,1)S(1)}, bf16[8,2,512]{2,1,0:T(2,128)(2,1)}, u32[]{:S(2)}) %copy-start.3) | copy-done | bytes 16408
  5.7 48.8 %prefix_attention_backward.1 = (bf16[128,2048]{1,0:T(8,128)(2,1)S(1)}, bf16[2,128,512]{2,1,0:T(8,128)(2,1)S(1)}, f32[2,8,512]{2,1,0:T(8,128)S(1)}) custom-call(bf16[128,2048]{1,0:T(8,128)(2,1)S(1)} %copy-done, bf16[2,128,512]{2,1,0:T(8,128)(2,1)S(1)} %copy-done.2, bf16[8,2,512]{2,1,0:T(2,128)(2,1)S(1)} %copy-done.3, bf16[128,2048]{1,0:T(8,128)(2,1)S(1)} %copy-done.1, ...), custom_call_target="tpu_custom_call" | custom-call | tf_op jit(solution)/shard_map/prefix_attention_backward/pallas_call | solution.py:375
  54.5 0.6 %copy.9 = bf16[8,2,512]{2,1,0:T(2,128)(2,1)} copy(bf16[8,2,512]{2,0,1:T(8,128)(2,1)S(1)} %convert_bitcast_fusion) | data formatting | bytes 32768
  55.1 0.8 %copy.14 = bf16[128,2048]{1,0:T(8,128)(2,1)} copy(bf16[128,2048]{1,0:T(8,128)(2,1)S(1)} %get-tuple-element.15) | data formatting | bytes 1048576
  55.9 0.7 %copy.15 = bf16[2,128,512]{2,1,0:T(8,128)(2,1)} copy(bf16[2,128,512]{2,1,0:T(8,128)(2,1)S(1)} %get-tuple-element.16) | data formatting | bytes 524288
  (1 shorter events, 0.0 us)
Async XLA Ops:
  1.9 1.0 %copy-start = (bf16[128,2048]{1,0:T(8,128)(2,1)S(1)}, bf16[128,2048]{1,0:T(8,128)(2,1)}, u32[]{:S(2)}) copy-start(bf16[128,2048]{1,0:T(8,128)(2,1)} %q_hbm.1) | copy-start | bytes 1572868
  3.0 1.0 %copy-start.1 = (bf16[128,2048]{1,0:T(8,128)(2,1)S(1)}, bf16[128,2048]{1,0:T(8,128)(2,1)}, u32[]{:S(2)}) copy-start(bf16[128,2048]{1,0:T(8,128)(2,1)} %do_hbm.1) | copy-start | bytes 1572868
  4.0 0.9 %copy-start.2 = (bf16[2,128,512]{2,1,0:T(8,128)(2,1)S(1)}, bf16[2,128,512]{2,1,0:T(8,128)(2,1)}, u32[]{:S(2)}) copy-start(bf16[2,128,512]{2,1,0:T(8,128)(2,1)} %rkv_hbm.1) | copy-start | bytes 786436
  5.0 0.7 %copy-start.3 = (bf16[8,2,512]{2,1,0:T(2,128)(2,1)S(1)}, bf16[8,2,512]{2,1,0:T(2,128)(2,1)}, u32[]{:S(2)}) copy-start(bf16[8,2,512]{2,1,0:T(2,128)(2,1)} %pkv_ref.1) | copy-start | bytes 49156

commit v2 on v1

v2 whole, which is shorter than its diff:
```python
import functools
import math

import jax
import jax.numpy as jnp
from jax import lax
from jax.experimental import pallas as pl
from jax.experimental.pallas import tpu as pltpu
from jax.sharding import PartitionSpec as P

HD = 128
GROUP = 4
NY = 4
NZ = 8
ROWS = 128
SCALE = 1.0 / math.sqrt(HD)
LOG2E = 1.4426950408889634
UNROLL = 4
MESH = pl.DeviceIdType.MESH
F32 = jnp.float32
BF16 = jnp.bfloat16
NT = (((1,), (1,)), ((), ()))
TN = (((0,), (0,)), ((), ()))


def dot(a, b, dims=(((1,), (0,)), ((), ()))):
    return lax.dot_general(a, b, dims, preferred_element_type=F32)


def kernel(
    q_hbm, rkv_hbm, pkv_hbm, do_hbm, len_hbm, rew_hbm,
    gq_ref, grkv_ref, gp_ref,
    gp_st, pkv_in, len_in, rew_in, kvblk, zrecv, kv_all, stat_own, statz, staty_own, staty,
    q_in, do_in, rkv_in, qcat, docat, e_sc, dp_sc, top_sc, sum_sc, dot_sc, p_sc, ds_sc, weights,
    ysend, yrecv, yown, zsend, zback, gq_st, grkv_st, gq_back, grkv_back,
    zs_sem, zr_sem, ss_sem, sr_sem, ys_sem, yr_sem, sys_sem, syr_sem,
    in_sem, xs_sem, xr_sem, rys_sem, ryr_sem, rzs_sem, rzr_sem, out_sem, os_sem, or_sem,
):
    group = lax.axis_index("group")
    index = lax.axis_index("rollout")
    y = index // (2 * NZ)
    z = (index // 2) % NZ
    core = index % 2
    other = 1 - core
    prefix = NY * NZ * 16

    def device(yy, zz, cc):
        return (group, (yy * NZ + zz) * 2 + cc)

    def remote(src, dst, ssem, rsem, where):
        return pltpu.make_async_remote_copy(
            src_ref=src, dst_ref=dst, send_sem=ssem, recv_sem=rsem,
            device_id=where, device_id_type=MESH,
        )

    column = [(d, e) for d in range(NZ) for e in range(2) if d or e]

    def peer(d, e):
        return device(y, z ^ d, core ^ e)

    barrier = pltpu.get_barrier_semaphore()
    for d, e in column:
        pl.semaphore_signal(barrier, inc=1, device_id=peer(d, e), device_id_type=MESH)
    for d in range(1, NY):
        pl.semaphore_signal(
            barrier, inc=1, device_id=device((y + d) % NY, z, core), device_id_type=MESH
        )

    my_q = pl.multiple_of(core * 1024, 1024)
    other_q = pl.multiple_of(other * 1024, 1024)
    my_kv = pl.multiple_of(core * 256, 256)
    other_kv = pl.multiple_of(other * 256, 256)
    loads = [
        pltpu.make_async_copy(q_hbm.at[:, pl.ds(my_q, 1024)], q_in.at[core], in_sem.at[0]),
        pltpu.make_async_copy(do_hbm.at[:, pl.ds(my_q, 1024)], do_in.at[core], in_sem.at[1]),
        pltpu.make_async_copy(rkv_hbm.at[:, :, pl.ds(my_kv, 256)], rkv_in.at[core], in_sem.at[2]),
    ]
    small = [
        pltpu.make_async_copy(pkv_hbm, pkv_in, in_sem.at[3]),
        pltpu.make_async_copy(len_hbm, len_in, in_sem.at[4]),
        pltpu.make_async_copy(rew_hbm, rew_in, in_sem.at[5]),
    ]
    for load in small + loads:
        load.start()
    for load in small:
        load.wait()

    pair = pkv_in[...].astype(F32)
    own_k = pair[:, 0, :]
    own_v = pair[:, 1, :]
    for hd in range(2):
        for cc in range(2):
            cols = slice(cc * 256 + hd * HD, cc * 256 + hd * HD + HD)
            kvblk[hd, cc] = jnp.concatenate([own_k[:, cols], own_v[:, cols]], axis=0).astype(BF16)
        zrecv[hd, z * 2 + core] = kvblk[hd, core]

    lane = lax.broadcasted_iota(jnp.int32, (1, 128), 1)
    reward = rew_in[0].astype(F32)
    length = len_in[0].astype(F32)
    stat = jnp.where(
        lane == 0, reward, jnp.where(lane == 1, reward * reward, jnp.where(lane == 2, length, 0.0))
    )
    stat_own[0] = stat
    statz[z * 2 + core] = stat

    pl.semaphore_wait(barrier, len(column) + NY - 1)

    zcopies = []

    def column_send(hd):
        for i, (d, e) in enumerate(column):
            zcopies.append(
                remote(
                    kvblk.at[hd, core ^ e], zrecv.at[hd, z * 2 + core], zs_sem.at[hd, i],
                    zr_sem.at[hd, d * 2 + e], peer(d, e),
                )
            )
            zcopies[-1].start()

    column_send(0)
    scopies = []
    for i, (d, e) in enumerate(column):
        scopies.append(
            remote(
                stat_own.at[0], statz.at[z * 2 + core], ss_sem.at[i], sr_sem.at[d * 2 + e], peer(d, e)
            )
        )
        scopies[-1].start()
    column_send(1)
    partner = device(y, z, other)
    xcopies = [
        remote(q_hbm.at[:, pl.ds(other_q, 1024)], q_in.at[core], xs_sem.at[0], xr_sem.at[0], partner),
        remote(
            rkv_hbm.at[:, :, pl.ds(other_kv, 256)], rkv_in.at[core], xs_sem.at[1], xr_sem.at[1], partner
        ),
        remote(do_hbm.at[:, pl.ds(other_q, 1024)], do_in.at[core], xs_sem.at[2], xr_sem.at[2], partner),
    ]
    for copy in xcopies:
        copy.start()

    ycopies = []

    def row_send(hd):
        for d in range(NZ):
            for e in range(2):
                if d or e:
                    slot = (z ^ d) * 2 + (core ^ e)
                    remote(
                        kvblk.at[hd, 0], zrecv.at[hd, slot], zs_sem.at[hd, 0], zr_sem.at[hd, d * 2 + e],
                        peer(d, e),
                    ).wait_recv()
            zz = z ^ d
            first = zrecv[hd, zz * 2].astype(F32)
            second = zrecv[hd, zz * 2 + 1].astype(F32)
            at = pl.ds(pl.multiple_of(zz * 16, 16), 16)
            kv_all[hd, 0, 0, at, :] = jnp.concatenate([first[:8], second[:8]], axis=0).astype(BF16)
            kv_all[hd, 1, 0, at, :] = jnp.concatenate([first[8:], second[8:]], axis=0).astype(BF16)
            for k in range(1, NY):
                copy = remote(
                    kv_all.at[hd, :, 0, at, :], kv_all.at[hd, :, k, at, :],
                    ys_sem.at[hd, d * (NY - 1) + k - 1], yr_sem.at[hd, k - 1],
                    device((y + k) % NY, z, core),
                )
                copy.start()
                ycopies.append(copy)

    def block(hd, slot):
        cols = slice(hd * HD, (hd + 1) * HD)

        def strip(s, carry):
            if slot == NY:
                k_rows = rkv_in[s // 2, 0, :, cols]
                v_rows = rkv_in[s // 2, 1, :, cols]
            else:
                k_rows = kv_all[hd, 0, slot]
                v_rows = kv_all[hd, 1, slot]
            scores = dot(k_rows, qcat[hd, s], NT)
            if slot == NY:
                key = lax.broadcasted_iota(jnp.int32, (ROWS, 256), 0)
                query = lax.broadcasted_iota(jnp.int32, (ROWS, 256), 1) % ROWS
                scores = jnp.where(key <= query, scores, -1e30)
            grad_soft = dot(v_rows, docat[hd, s], NT)
            top = jnp.max(scores, axis=0, keepdims=True)
            powers = jnp.exp2((scores - top) * (SCALE * LOG2E))
            e_sc[hd, s, slot] = powers
            dp_sc[hd, s, slot] = grad_soft
            top_sc[hd, s, slot] = top
            sum_sc[hd, s, slot] = jnp.sum(powers, axis=0, keepdims=True)
            dot_sc[hd, s, slot] = jnp.sum(powers * grad_soft, axis=0, keepdims=True)
            return carry

        lax.fori_loop(0, 4, strip, 0, unroll=UNROLL)

    for load in loads:
        load.wait()
    for copy in xcopies:
        copy.wait_recv()
    for hd in range(2):
        for j in range(2):
            for g in range(GROUP):
                col = hd * 512 + g * HD
                at = slice((g % 2) * ROWS, (g % 2 + 1) * ROWS)
                qcat[hd, 2 * j + g // 2, at, :] = q_in[j, :, col : col + HD]
                docat[hd, 2 * j + g // 2, at, :] = do_in[j, :, col : col + HD]
    block(0, NY)
    block(1, NY)
    row_send(0)
    for i, (d, e) in enumerate(column):
        slot = (z ^ d) * 2 + (core ^ e)
        remote(
            stat_own.at[0], statz.at[slot], ss_sem.at[0], sr_sem.at[d * 2 + e], peer(d, e)
        ).wait_recv()
    column_sum = jnp.sum(statz[...], axis=0)
    staty_own[0] = column_sum
    staty[y] = column_sum
    sycopies = []
    for k in range(1, NY):
        copy = remote(
            staty_own.at[0], staty.at[y], sys_sem.at[k - 1], syr_sem.at[k - 1],
            device((y + k) % NY, z, core),
        )
        copy.start()
        sycopies.append(copy)

    row_send(1)
    block(0, 0)
    block(1, 0)

    def row_wait(hd, k):
        remote(
            kv_all.at[hd, :, 0], kv_all.at[hd, :, k], ys_sem.at[hd, 0], yr_sem.at[hd, k - 1],
            device((y + NY - k) % NY, z, core),
        ).wait_recv()

    for k in (1, 3, 2):
        row_wait(0, k)
        block(0, k)

    for k in range(1, NY):
        yy = (y + NY - k) % NY
        remote(
            staty_own.at[0], staty.at[yy], sys_sem.at[0], syr_sem.at[k - 1], device(yy, z, core)
        ).wait_recv()
    totals = jnp.sum(staty[...], axis=0)
    rollouts = float(2 * NY * NZ)
    mean = totals[:, 0:1] / rollouts
    var = totals[:, 1:2] / rollouts - mean * mean
    divisor = jnp.sqrt(var) + 1.0
    norm = float(2 * NY * NZ * ROWS) / totals[:, 2:3]
    step = (lax.broadcasted_iota(jnp.int32, (1, 256), 1) % ROWS).astype(F32)
    for j in range(2):
        own = statz[z * 2 + j]
        weight = (own[:, 0:1] - mean) / divisor * norm
        weights[j] = jnp.where(step < own[:, 2:3], weight, 0.0)

    def finish(hd):
        def strip(s, carry):
            tops = [top_sc[hd, s, b] for b in range(NY + 1)]
            top = functools.reduce(jnp.maximum, tops)
            factors = [jnp.exp2((t - top) * (SCALE * LOG2E)) for t in tops]
            total = sum(sum_sc[hd, s, b] * factors[b] for b in range(NY + 1))
            inverse = 1.0 / total
            row_dot = sum(dot_sc[hd, s, b] * factors[b] for b in range(NY + 1)) * inverse
            scaled = weights[s // 2] * inverse
            at = pl.ds(pl.multiple_of(s * 256, 256), 256)
            for b in range(NY + 1):
                soft = e_sc[hd, s, b] * (factors[b] * scaled)
                rows = slice(b * ROWS, (b + 1) * ROWS)
                p_sc[hd, rows, at] = soft.astype(BF16)
                ds_sc[hd, rows, at] = (soft * (dp_sc[hd, s, b] - row_dot)).astype(BF16)
            return carry

        lax.fori_loop(0, 4, strip, 0, unroll=4)

    rycopies = []

    def prefix_grads(hd, kind):
        held, rows = (ds_sc, qcat) if kind == 0 else (p_sc, docat)
        grad = dot(held[hd, :prefix, :], rows[hd].reshape(1024, HD))
        if kind == 0:
            grad = grad * SCALE
        yown[hd, kind] = grad[:ROWS]
        for k in range(1, NY):
            ysend[hd, kind, k - 1] = grad[k * ROWS : (k + 1) * ROWS].astype(BF16)
            copy = remote(
                ysend.at[hd, kind, k - 1], yrecv.at[hd, kind, k - 1], rys_sem.at[hd, kind, k - 1],
                ryr_sem.at[hd, kind, k - 1], device((y + NY - k) % NY, z, core),
            )
            copy.start()
            rycopies.append(copy)

    def local_grads(hd):
        cols = slice(hd * HD, (hd + 1) * HD)
        for j in range(2):
            qs = qcat[hd, 2 * j : 2 * j + 2].reshape(512, HD)
            dos = docat[hd, 2 * j : 2 * j + 2].reshape(512, HD)
            at = slice(j * 512, j * 512 + 512)
            grkv_st[j, 0, :, cols] = (dot(ds_sc[hd, prefix:, at], qs) * SCALE).astype(BF16)
            grkv_st[j, 1, :, cols] = dot(p_sc[hd, prefix:, at], dos).astype(BF16)

        def query_strip(s, carry):
            j = s // 2
            at = pl.ds(pl.multiple_of(s * 256, 256), 256)
            kp = kv_all[hd, 0].reshape(prefix, HD)
            ko = rkv_in[j, 0, :, cols]
            grad = dot(kp, ds_sc[hd, :prefix, at], TN) + dot(ko, ds_sc[hd, prefix:, at], TN)
            grad = (grad * SCALE).T.astype(BF16)
            for g in range(2):
                col = pl.multiple_of(hd * 512 + (s % 2) * 256 + g * HD, HD)
                gq_st[j, :, pl.ds(col, HD)] = grad[g * ROWS : (g + 1) * ROWS]
            return carry

        lax.fori_loop(0, 4, query_strip, 0, unroll=UNROLL)

    rzcopies = []

    def row_sums(hd):
        for k in range(1, NY):
            for kind in range(2):
                remote(
                    ysend.at[hd, kind, k - 1], yrecv.at[hd, kind, k - 1], rys_sem.at[hd, kind, k - 1],
                    ryr_sem.at[hd, kind, k - 1], device((y + k) % NY, z, core),
                ).wait_recv()
        sums = [
            yown[hd, i]
            + (yrecv[hd, i, 0].astype(F32) + yrecv[hd, i, 1].astype(F32) + yrecv[hd, i, 2].astype(F32))
            for i in range(2)
        ]
        for zz in range(NZ):
            for cc in range(2):
                at = slice(zz * 16 + cc * 8, zz * 16 + cc * 8 + 8)
                zsend[hd, zz * 2 + cc] = jnp.concatenate([sums[0][at], sums[1][at]], axis=0).astype(BF16)
        zback[hd, z * 2 + core] = zsend[hd, z * 2 + core]
        for i, (d, e) in enumerate(column):
            copy = remote(
                zsend.at[hd, (z ^ d) * 2 + (core ^ e)], zback.at[hd, z * 2 + core],
                rzs_sem.at[hd, i], rzr_sem.at[hd, d * 2 + e], peer(d, e),
            )
            copy.start()
            rzcopies.append(copy)

    for hd in range(2):
        if hd == 1:
            for k in (1, 3, 2):
                row_wait(1, k)
                block(1, k)
        finish(hd)
        prefix_grads(hd, 1)
        prefix_grads(hd, 0)
    row_sums(0)
    local_grads(0)
    local_grads(1)
    outs = [
        pltpu.make_async_copy(gq_st.at[core], gq_ref.at[:, pl.ds(my_q, 1024)], out_sem.at[0]),
        pltpu.make_async_copy(grkv_st.at[core], grkv_ref.at[:, :, pl.ds(my_kv, 256)], out_sem.at[1]),
    ]
    ocopies = [
        remote(gq_st.at[other], gq_back, os_sem.at[0], or_sem.at[0], partner),
        remote(grkv_st.at[other], grkv_back, os_sem.at[1], or_sem.at[1], partner),
    ]
    for copy in ocopies + outs:
        copy.start()
    row_sums(1)
    backs = [
        pltpu.make_async_copy(gq_back, gq_ref.at[:, pl.ds(other_q, 1024)], out_sem.at[3]),
        pltpu.make_async_copy(grkv_back, grkv_ref.at[:, :, pl.ds(other_kv, 256)], out_sem.at[4]),
    ]
    for copy, back in zip(ocopies, backs):
        copy.wait_recv()
        back.start()
    outs = outs + backs

    for hd in range(2):
        for d, e in column:
            slot = (z ^ d) * 2 + (core ^ e)
            remote(
                zsend.at[hd, slot], zback.at[hd, slot], rzs_sem.at[hd, 0],
                rzr_sem.at[hd, d * 2 + e], peer(d, e),
            ).wait_recv()
    for cc in range(2):
        for hd in range(2):
            total = zback[hd, cc].astype(F32)
            for zz in range(1, NZ):
                total = total + zback[hd, zz * 2 + cc].astype(F32)
            cols = slice(cc * 256 + hd * HD, cc * 256 + (hd + 1) * HD)
            gp_st[0, :, cols] = total[:8]
            gp_st[1, :, cols] = total[8:]
    outs.append(pltpu.make_async_copy(gp_st, gp_ref, out_sem.at[2]))
    outs[-1].start()

    for copy in outs:
        copy.wait()
    for copy in ocopies + zcopies + scopies + xcopies + ycopies + sycopies + rycopies + rzcopies:
        copy.wait_send()


def emit(gq_from, grkv_from, gp_from, gq_to, grkv_to, gp_to, sums, pairs, gq, grkv, fetch_sem, put_sem):
    ways = [(gp_from, sums, None), (grkv_from, grkv, grkv_to)]
    for i in range(4):
        at = pl.ds(i * 32, 32)
        ways.append((gq_from.at[at], gq.at[at], gq_to.at[at]))
    fetches = [pltpu.make_async_copy(way[0], way[1], fetch_sem.at[i]) for i, way in enumerate(ways)]
    for fetch in fetches:
        fetch.start()
    fetches[0].wait()
    pairs[...] = jnp.stack([sums[0], sums[1]], axis=1).astype(BF16)
    puts = [pltpu.make_async_copy(pairs, gp_to, put_sem.at[0])]
    puts[0].start()
    for i in range(1, len(ways)):
        fetches[i].wait()
        puts.append(pltpu.make_async_copy(ways[i][1], ways[i][2], put_sem.at[i]))
        puts[i].start()
    for put in puts:
        put.wait()


def local(queries, roll_kv, prefix_kv, grad_seed, lengths, rewards):
    prefix = NY * NZ * 16
    keys = prefix + ROWS
    near = NZ * 16
    vmem = pltpu.VMEM
    sem = pltpu.SemaphoreType.DMA
    hbm = pl.BlockSpec(memory_space=pltpu.HBM)
    ncol = 2 * NZ
    grads = pl.pallas_call(
        kernel,
        out_shape=(
            jax.ShapeDtypeStruct(queries.shape, BF16),
            jax.ShapeDtypeStruct(roll_kv.shape, BF16),
            jax.ShapeDtypeStruct((2, 8, 512), F32),
        ),
        in_specs=[hbm] * 6,
        out_specs=(hbm, hbm, hbm),
        scratch_shapes=[
            vmem((2, 8, 512), F32),
            vmem(prefix_kv.shape, BF16),
            pltpu.SMEM((1,), jnp.int32),
            pltpu.SMEM((1,), jnp.int32),
            vmem((2, 2, 16, HD), BF16),
            vmem((2, ncol, 16, HD), BF16),
            vmem((2, 2, NY, near, HD), BF16),
            vmem((1, 1, 128), F32),
            vmem((ncol, 1, 128), F32),
            vmem((1, 1, 128), F32),
            vmem((NY, 1, 128), F32),
            vmem((2, ROWS, 1024), BF16),
            vmem((2, ROWS, 1024), BF16),
            vmem((2, 2, ROWS, 256), BF16),
            vmem((2, 4, 256, HD), BF16),
            vmem((2, 4, 256, HD), BF16),
            vmem((2, 4, NY + 1, ROWS, 256), F32),
            vmem((2, 4, NY + 1, ROWS, 256), F32),
            vmem((2, 4, NY + 1, 1, 256), F32),
            vmem((2, 4, NY + 1, 1, 256), F32),
            vmem((2, 4, NY + 1, 1, 256), F32),
            vmem((2, keys, 1024), BF16),
            vmem((2, keys, 1024), BF16),
            vmem((2, 1, 256), F32),
            vmem((2, 2, NY - 1, near, HD), BF16),
            vmem((2, 2, NY - 1, near, HD), BF16),
            vmem((2, 2, near, HD), F32),
            vmem((2, ncol, 16, HD), BF16),
            vmem((2, ncol, 16, HD), BF16),
            vmem((2, ROWS, 1024), BF16),
            vmem((2, 2, ROWS, 256), BF16),
            vmem((ROWS, 1024), BF16),
            vmem((2, ROWS, 256), BF16),
            sem((2, ncol)), sem((2, ncol)),
            sem((ncol,)), sem((ncol,)),
            sem((2, NZ * (NY - 1))), sem((2, NY - 1)),
            sem((NY - 1,)), sem((NY - 1,)),
            sem((6,)), sem((3,)), sem((3,)),
            sem((2, 2, NY - 1)), sem((2, 2, NY - 1)),
            sem((2, ncol)), sem((2, ncol)),
            sem((5,)), sem((2,)), sem((2,)),
        ],
        compiler_params=pltpu.CompilerParams(
            collective_id=0, has_side_effects=True, vmem_limit_bytes=60 * 2**20
        ),
        name="prefix_attention_backward",
    )(queries, roll_kv, prefix_kv, grad_seed, lengths, rewards)
    return pl.pallas_call(
        emit,
        out_shape=(
            jax.ShapeDtypeStruct(queries.shape, BF16),
            jax.ShapeDtypeStruct(roll_kv.shape, BF16),
            jax.ShapeDtypeStruct(prefix_kv.shape, BF16),
        ),
        in_specs=[hbm] * 3,
        out_specs=[hbm] * 3,
        scratch_shapes=[
            vmem((2, 8, 512), F32), vmem(prefix_kv.shape, BF16), vmem(queries.shape, BF16),
            vmem(roll_kv.shape, BF16), sem((6,)), sem((6,)),
        ],
        compiler_params=pltpu.CompilerParams(vmem_limit_bytes=60 * 2**20),
        name="emit",
    )(*grads)


def solution(mesh):
    rows = ("group", "rollout")
    return jax.shard_map(
        local,
        mesh=mesh,
        in_specs=(
            P(rows, None), P(None, rows, None), P(rows, None, None), P(rows, None), P(rows), P(rows),
        ),
        out_specs=(P(rows, None), P(None, rows, None), P(rows, None, None)),
        check_vma=False,
    )
```

time: 56.9 us -> 48.9 us (0.86)
  local copies, waits for them, and re-layouts: 5.86 us -> 0 us
  Pallas kernels: 48.8 us -> 46.7 us
    unnamed x11 -> x0, local copies, waits for them, and re-layouts: 5.86 us -> none
    pallas_call x1, Pallas kernels: 48.8 us -> 44.8 us  [local(): pl.pallas_call(kernel, out_shape=(jax.ShapeDtypeStruct(queries.shape, BF1...]
    pallas_call x0 -> x1, Pallas kernels: none -> 1.94 us  [local(): pl.pallas_call(emit, out_shape=(jax.ShapeDtypeStruct(queries.shape, BF16)...]
where the time goes in v2:
time: 48.9 us; the launch traced here: 48.7 us
  Pallas kernels  46.7 us (96%)
  between operations  1.93 us (4%)
    pallas_call x1, Pallas kernels, local(): pl.pallas_call(kernel, out_shape=(jax.ShapeDtypeStruct(queries.shape, BF1...  44.8 us
    pallas_call x1, Pallas kernels, local(): pl.pallas_call(emit, out_shape=(jax.ShapeDtypeStruct(queries.shape, BF16)...  1.94 us

profile of v2, /device:TPU:1, one launch (start us, length us, event | category | flops | bytes accessed | tf_op | source)
XLA Modules:
  0.0 48.7 jit_solution(15691081224710562754)
XLA Ops:
  1.9 44.8 %prefix_attention_backward.1 = (bf16[128,2048]{1,0:T(8,128)(2,1)}, bf16[2,128,512]{2,1,0:T(8,128)(2,1)}, f32[2,8,512]{2,1,0:T(8,128)}) custom-call(bf16[128,2048]{1,0:T(8,128)(2,1)} %q_hbm.1, bf16[2,128,512]{2,1,0:T(8,128)(2,1)} %rkv_hbm.1, bf16[8,2,512]{2,1,0:T(2,128)(2,1)} %pkv_hbm.1, bf16[128,2048]{1,0:T(8,128)(2,1)} %do_hbm.1, s32[1]{0:T(128)S(6)} %copy.9.len_hbm, ...), custom_call_target="tpu_custom_call" | custom-call | tf_op jit(solution)/shard_map/prefix_attention_backward/pallas_call | solution.py:425
  46.7 1.9 %emit.1 = (bf16[128,2048]{1,0:T(8,128)(2,1)}, bf16[2,128,512]{2,1,0:T(8,128)(2,1)}, bf16[8,2,512]{2,1,0:T(2,128)(2,1)}) custom-call(bf16[128,2048]{1,0:T(8,128)(2,1)} %get-tuple-element.6.gq_from, bf16[2,128,512]{2,1,0:T(8,128)(2,1)} %get-tuple-element.7.grkv_from, f32[2,8,512]{2,1,0:T(8,128)} %get-tuple-element.8.gp_from), custom_call_target="tpu_custom_call" | custom-call | tf_op jit(solution)/shard_map/emit/pallas_call | solution.py:482

commit v3 on v2

--- a/solution.py
+++ b/solution.py
@@ -53,7 +53,7 @@
             device_id=where, device_id_type=MESH,
         )
 
-    column = [(d, e) for d in range(NZ) for e in range(2) if d or e]
+    column = [(d, e) for d in reversed(range(NZ)) for e in range(2) if d or e]
 
     def peer(d, e):
         return device(y, z ^ d, core ^ e)
@@ -105,27 +105,16 @@
 
     pl.semaphore_wait(barrier, len(column) + NY - 1)
 
-    zcopies = []
-
     def column_send(hd):
-        for i, (d, e) in enumerate(column):
-            zcopies.append(
-                remote(
-                    kvblk.at[hd, core ^ e], zrecv.at[hd, z * 2 + core], zs_sem.at[hd, i],
-                    zr_sem.at[hd, d * 2 + e], peer(d, e),
-                )
-            )
-            zcopies[-1].start()
+        for d, e in column:
+            remote(
+                kvblk.at[hd, core ^ e], zrecv.at[hd, z * 2 + core], zs_sem.at[0], zr_sem.at[hd, d],
+                peer(d, e),
+            ).start()
 
     column_send(0)
-    scopies = []
-    for i, (d, e) in enumerate(column):
-        scopies.append(
-            remote(
-                stat_own.at[0], statz.at[z * 2 + core], ss_sem.at[i], sr_sem.at[d * 2 + e], peer(d, e)
-            )
-        )
-        scopies[-1].start()
+    for d, e in column:
+        remote(stat_own.at[0], statz.at[z * 2 + core], ss_sem.at[0], sr_sem.at[0], peer(d, e)).start()
     column_send(1)
     partner = device(y, z, other)
     xcopies = [
@@ -138,31 +127,21 @@
     for copy in xcopies:
         copy.start()
 
-    ycopies = []
-
     def row_send(hd):
         for d in range(NZ):
-            for e in range(2):
-                if d or e:
-                    slot = (z ^ d) * 2 + (core ^ e)
-                    remote(
-                        kvblk.at[hd, 0], zrecv.at[hd, slot], zs_sem.at[hd, 0], zr_sem.at[hd, d * 2 + e],
-                        peer(d, e),
-                    ).wait_recv()
             zz = z ^ d
+            landed = zrecv.at[hd, pl.ds(zz * 2, 2)] if d else zrecv.at[hd, pl.ds(z * 2 + other, 1)]
+            remote(landed, landed, zs_sem.at[0], zr_sem.at[hd, d], peer(d or 1, 0)).wait_recv()
             first = zrecv[hd, zz * 2].astype(F32)
             second = zrecv[hd, zz * 2 + 1].astype(F32)
             at = pl.ds(pl.multiple_of(zz * 16, 16), 16)
             kv_all[hd, 0, 0, at, :] = jnp.concatenate([first[:8], second[:8]], axis=0).astype(BF16)
             kv_all[hd, 1, 0, at, :] = jnp.concatenate([first[8:], second[8:]], axis=0).astype(BF16)
-            for k in range(1, NY):
-                copy = remote(
-                    kv_all.at[hd, :, 0, at, :], kv_all.at[hd, :, k, at, :],
-                    ys_sem.at[hd, d * (NY - 1) + k - 1], yr_sem.at[hd, k - 1],
-                    device((y + k) % NY, z, core),
-                )
-                copy.start()
-                ycopies.append(copy)
+            for k in (2, 1, 3):
+                remote(
+                    kv_all.at[hd, :, 0, at, :], kv_all.at[hd, :, k, at, :], ys_sem.at[0],
+                    yr_sem.at[hd, k - 1], device((y + k) % NY, z, core),
+                ).start()
 
     def block(hd, slot):
         cols = slice(hd * HD, (hd + 1) * HD)
@@ -205,22 +184,16 @@
     block(0, NY)
     block(1, NY)
     row_send(0)
-    for i, (d, e) in enumerate(column):
-        slot = (z ^ d) * 2 + (core ^ e)
-        remote(
-            stat_own.at[0], statz.at[slot], ss_sem.at[0], sr_sem.at[d * 2 + e], peer(d, e)
-        ).wait_recv()
+    all_but_one = statz.at[pl.ds(0, len(column))]
+    stats = remote(all_but_one, all_but_one, ss_sem.at[0], sr_sem.at[0], peer(1, 0))
+    stats.wait_recv()
     column_sum = jnp.sum(statz[...], axis=0)
     staty_own[0] = column_sum
     staty[y] = column_sum
-    sycopies = []
     for k in range(1, NY):
-        copy = remote(
-            staty_own.at[0], staty.at[y], sys_sem.at[k - 1], syr_sem.at[k - 1],
-            device((y + k) % NY, z, core),
-        )
-        copy.start()
-        sycopies.append(copy)
+        remote(
+            staty_own.at[0], staty.at[y], sys_sem.at[0], syr_sem.at[0], device((y + k) % NY, z, core)
+        ).start()
 
     row_send(1)
     block(0, 0)
@@ -228,7 +201,7 @@
 
     def row_wait(hd, k):
         remote(
-            kv_all.at[hd, :, 0], kv_all.at[hd, :, k], ys_sem.at[hd, 0], yr_sem.at[hd, k - 1],
+            kv_all.at[hd, :, 0], kv_all.at[hd, :, k], ys_sem.at[0], yr_sem.at[hd, k - 1],
             device((y + NY - k) % NY, z, core),
         ).wait_recv()
 
@@ -236,11 +209,10 @@
         row_wait(0, k)
         block(0, k)
 
-    for k in range(1, NY):
-        yy = (y + NY - k) % NY
-        remote(
-            staty_own.at[0], staty.at[yy], sys_sem.at[0], syr_sem.at[k - 1], device(yy, z, core)
-        ).wait_recv()
+    next_row = device((y + 1) % NY, z, core)
+    other_rows = staty.at[pl.ds(0, NY - 1)]
+    row_stats = remote(other_rows, other_rows, sys_sem.at[0], syr_sem.at[0], next_row)
+    row_stats.wait_recv()
     totals = jnp.sum(staty[...], axis=0)
     rollouts = float(2 * NY * NZ)
     mean = totals[:, 0:1] / rollouts
@@ -272,22 +244,18 @@
 
         lax.fori_loop(0, 4, strip, 0, unroll=4)
 
-    rycopies = []
-
     def prefix_grads(hd, kind):
         held, rows = (ds_sc, qcat) if kind == 0 else (p_sc, docat)
         grad = dot(held[hd, :prefix, :], rows[hd].reshape(1024, HD))
         if kind == 0:
             grad = grad * SCALE
         yown[hd, kind] = grad[:ROWS]
-        for k in range(1, NY):
+        for k in (2, 1, 3):
             ysend[hd, kind, k - 1] = grad[k * ROWS : (k + 1) * ROWS].astype(BF16)
-            copy = remote(
-                ysend.at[hd, kind, k - 1], yrecv.at[hd, kind, k - 1], rys_sem.at[hd, kind, k - 1],
-                ryr_sem.at[hd, kind, k - 1], device((y + NY - k) % NY, z, core),
-            )
-            copy.start()
-            rycopies.append(copy)
+            remote(
+                ysend.at[hd, kind, k - 1], yrecv.at[hd, kind, k - 1], rys_sem.at[0], ryr_sem.at[hd],
+                device((y + NY - k) % NY, z, core),
+            ).start()
 
     def local_grads(hd):
         cols = slice(hd * HD, (hd + 1) * HD)
@@ -312,15 +280,8 @@
 
         lax.fori_loop(0, 4, query_strip, 0, unroll=UNROLL)
 
-    rzcopies = []
-
     def row_sums(hd):
-        for k in range(1, NY):
-            for kind in range(2):
-                remote(
-                    ysend.at[hd, kind, k - 1], yrecv.at[hd, kind, k - 1], rys_sem.at[hd, kind, k - 1],
-                    ryr_sem.at[hd, kind, k - 1], device((y + k) % NY, z, core),
-                ).wait_recv()
+        remote(ysend.at[hd], yrecv.at[hd], rys_sem.at[0], ryr_sem.at[hd], next_row).wait_recv()
         sums = [
             yown[hd, i]
             + (yrecv[hd, i, 0].astype(F32) + yrecv[hd, i, 1].astype(F32) + yrecv[hd, i, 2].astype(F32))
@@ -331,13 +292,11 @@
                 at = slice(zz * 16 + cc * 8, zz * 16 + cc * 8 + 8)
                 zsend[hd, zz * 2 + cc] = jnp.concatenate([sums[0][at], sums[1][at]], axis=0).astype(BF16)
         zback[hd, z * 2 + core] = zsend[hd, z * 2 + core]
-        for i, (d, e) in enumerate(column):
-            copy = remote(
-                zsend.at[hd, (z ^ d) * 2 + (core ^ e)], zback.at[hd, z * 2 + core],
-                rzs_sem.at[hd, i], rzr_sem.at[hd, d * 2 + e], peer(d, e),
-            )
-            copy.start()
-            rzcopies.append(copy)
+        for d, e in column:
+            remote(
+                zsend.at[hd, (z ^ d) * 2 + (core ^ e)], zback.at[hd, z * 2 + core], rzs_sem.at[0],
+                rzr_sem.at[hd], peer(d, e),
+            ).start()
 
     for hd in range(2):
         if hd == 1:
@@ -347,7 +306,6 @@
         finish(hd)
         prefix_grads(hd, 1)
         prefix_grads(hd, 0)
-    row_sums(0)
     local_grads(0)
     local_grads(1)
     outs = [
@@ -360,6 +318,7 @@
     ]
     for copy in ocopies + outs:
         copy.start()
+    row_sums(0)
     row_sums(1)
     backs = [
         pltpu.make_async_copy(gq_back, gq_ref.at[:, pl.ds(other_q, 1024)], out_sem.at[3]),
@@ -371,12 +330,8 @@
     outs = outs + backs
 
     for hd in range(2):
-        for d, e in column:
-            slot = (z ^ d) * 2 + (core ^ e)
-            remote(
-                zsend.at[hd, slot], zback.at[hd, slot], rzs_sem.at[hd, 0],
-                rzr_sem.at[hd, d * 2 + e], peer(d, e),
-            ).wait_recv()
+        landed = zback.at[hd, pl.ds(0, len(column))]
+        remote(landed, landed, rzs_sem.at[0], rzr_sem.at[hd], peer(1, 0)).wait_recv()
     for cc in range(2):
         for hd in range(2):
             total = zback[hd, cc].astype(F32)
@@ -390,8 +345,17 @@
 
     for copy in outs:
         copy.wait()
-    for copy in ocopies + zcopies + scopies + xcopies + ycopies + sycopies + rycopies + rzcopies:
+    for copy in ocopies + xcopies:
         copy.wait_send()
+    stats.wait_send()
+    row_stats.wait_send()
+    for held, sem in (
+        (zrecv.at[:, pl.ds(0, len(column))], zs_sem.at[0]),
+        (kv_all.at[:, :, pl.ds(1, NY - 1)], ys_sem.at[0]),
+        (ysend, rys_sem.at[0]),
+        (zsend.at[:, pl.ds(0, len(column))], rzs_sem.at[0]),
+    ):
+        remote(held, held, sem, sem, next_row).wait_send()
 
 
 def emit(gq_from, grkv_from, gp_from, gq_to, grkv_to, gp_to, sums, pairs, gq, grkv, fetch_sem, put_sem):
@@ -465,13 +429,13 @@
             vmem((2, 2, ROWS, 256), BF16),
             vmem((ROWS, 1024), BF16),
             vmem((2, ROWS, 256), BF16),
-            sem((2, ncol)), sem((2, ncol)),
-            sem((ncol,)), sem((ncol,)),
-            sem((2, NZ * (NY - 1))), sem((2, NY - 1)),
-            sem((NY - 1,)), sem((NY - 1,)),
+            sem((1,)), sem((2, NZ)),
+            sem((1,)), sem((1,)),
+            sem((1,)), sem((2, NY - 1)),
+            sem((1,)), sem((1,)),
             sem((6,)), sem((3,)), sem((3,)),
-            sem((2, 2, NY - 1)), sem((2, 2, NY - 1)),
-            sem((2, ncol)), sem((2, ncol)),
+            sem((1,)), sem((2,)),
+            sem((1,)), sem((2,)),
             sem((5,)), sem((2,)), sem((2,)),
         ],
         compiler_params=pltpu.CompilerParams(

time: 48.9 us -> 45.6 us (0.933)
  Pallas kernels: 46.7 us -> 43.4 us
    pallas_call x1, Pallas kernels: 44.8 us -> 41.5 us  [local(): pl.pallas_call(kernel, out_shape=(jax.ShapeDtypeStruct(queries.shape, BF1...]
where the time goes in v3:
time: 45.6 us; the launch traced here: 45.4 us
  Pallas kernels  43.4 us (95%)
  between operations  1.93 us (4%)
    pallas_call x1, Pallas kernels, local(): pl.pallas_call(kernel, out_shape=(jax.ShapeDtypeStruct(queries.shape, BF1...  41.5 us
    pallas_call x1, Pallas kernels, local(): pl.pallas_call(emit, out_shape=(jax.ShapeDtypeStruct(queries.shape, BF16)...  1.94 us

profile of v3, /device:TPU:1, one launch (start us, length us, event | category | flops | bytes accessed | tf_op | source)
XLA Modules:
  0.0 45.4 jit_solution(10874234887168310345)
XLA Ops:
  1.9 41.5 %prefix_attention_backward.1 = (bf16[128,2048]{1,0:T(8,128)(2,1)}, bf16[2,128,512]{2,1,0:T(8,128)(2,1)}, f32[2,8,512]{2,1,0:T(8,128)}) custom-call(bf16[128,2048]{1,0:T(8,128)(2,1)} %q_hbm.1, bf16[2,128,512]{2,1,0:T(8,128)(2,1)} %rkv_hbm.1, bf16[8,2,512]{2,1,0:T(2,128)(2,1)} %pkv_hbm.1, bf16[128,2048]{1,0:T(8,128)(2,1)} %do_hbm.1, s32[1]{0:T(128)S(6)} %copy.9.len_hbm, ...), custom_call_target="tpu_custom_call" | custom-call | tf_op jit(solution)/shard_map/prefix_attention_backward/pallas_call | solution.py:389
  43.4 1.9 %emit.1 = (bf16[128,2048]{1,0:T(8,128)(2,1)}, bf16[2,128,512]{2,1,0:T(8,128)(2,1)}, bf16[8,2,512]{2,1,0:T(2,128)(2,1)}) custom-call(bf16[128,2048]{1,0:T(8,128)(2,1)} %get-tuple-element.6.gq_from, bf16[2,128,512]{2,1,0:T(8,128)(2,1)} %get-tuple-element.7.grkv_from, f32[2,8,512]{2,1,0:T(8,128)} %get-tuple-element.8.gp_from), custom_call_target="tpu_custom_call" | custom-call | tf_op jit(solution)/shard_map/emit/pallas_call | solution.py:446

commit v4 on v3

--- a/solution.py
+++ b/solution.py
@@ -29,10 +29,10 @@
 
 def kernel(
     q_hbm, rkv_hbm, pkv_hbm, do_hbm, len_hbm, rew_hbm,
-    gq_ref, grkv_ref, gp_ref,
-    gp_st, pkv_in, len_in, rew_in, kvblk, zrecv, kv_all, stat_own, statz, staty_own, staty,
+    gq_ref, grkv_ref, zback,
+    pkv_in, len_in, rew_in, kvblk, zrecv, kv_all, stat_own, statz, staty_own, staty,
     q_in, do_in, rkv_in, qcat, docat, e_sc, dp_sc, top_sc, sum_sc, dot_sc, p_sc, ds_sc, weights,
-    ysend, yrecv, yown, zsend, zback, gq_st, grkv_st, gq_back, grkv_back,
+    ysend, yrecv, yown, zsend, gq_st, grkv_st, gq_back, grkv_back,
     zs_sem, zr_sem, ss_sem, sr_sem, ys_sem, yr_sem, sys_sem, syr_sem,
     in_sem, xs_sem, xr_sem, rys_sem, ryr_sem, rzs_sem, rzr_sem, out_sem, os_sem, or_sem,
 ):
@@ -54,12 +54,14 @@
         )
 
     column = [(d, e) for d in reversed(range(NZ)) for e in range(2) if d or e]
+    half = NZ // 2
+    close = [(d, e) for d, e in column if d <= half]
 
     def peer(d, e):
         return device(y, z ^ d, core ^ e)
 
     barrier = pltpu.get_barrier_semaphore()
-    for d, e in column:
+    for d, e in close:
         pl.semaphore_signal(barrier, inc=1, device_id=peer(d, e), device_id_type=MESH)
     for d in range(1, NY):
         pl.semaphore_signal(
@@ -103,18 +105,20 @@
     stat_own[0] = stat
     statz[z * 2 + core] = stat
 
-    pl.semaphore_wait(barrier, len(column) + NY - 1)
+    pl.semaphore_wait(barrier, len(close) + NY - 1)
 
     def column_send(hd):
-        for d, e in column:
+        for d, e in close:
             remote(
                 kvblk.at[hd, core ^ e], zrecv.at[hd, z * 2 + core], zs_sem.at[0], zr_sem.at[hd, d],
                 peer(d, e),
             ).start()
 
     column_send(0)
-    for d, e in column:
-        remote(stat_own.at[0], statz.at[z * 2 + core], ss_sem.at[0], sr_sem.at[0], peer(d, e)).start()
+    for d, e in close:
+        remote(
+            stat_own.at[0], statz.at[z * 2 + core], ss_sem.at[0], sr_sem.at[d // half], peer(d, e)
+        ).start()
     column_send(1)
     partner = device(y, z, other)
     xcopies = [
@@ -131,7 +135,8 @@
         for d in range(NZ):
             zz = z ^ d
             landed = zrecv.at[hd, pl.ds(zz * 2, 2)] if d else zrecv.at[hd, pl.ds(z * 2 + other, 1)]
-            remote(landed, landed, zs_sem.at[0], zr_sem.at[hd, d], peer(d or 1, 0)).wait_recv()
+            if d != half:
+                remote(landed, landed, zs_sem.at[0], zr_sem.at[hd, d], peer(d or 1, 0)).wait_recv()
             first = zrecv[hd, zz * 2].astype(F32)
             second = zrecv[hd, zz * 2 + 1].astype(F32)
             at = pl.ds(pl.multiple_of(zz * 16, 16), 16)
@@ -183,10 +188,25 @@
                 docat[hd, 2 * j + g // 2, at, :] = do_in[j, :, col : col + HD]
     block(0, NY)
     block(1, NY)
+    mirror = pl.ds((z ^ half) * 2, 2)
+
+    def pass_on(hd):
+        block_pair = zrecv.at[hd, mirror]
+        remote(block_pair, block_pair, zs_sem.at[0], zr_sem.at[hd, half], peer(half, 0)).wait_recv()
+        for d in reversed(range(1, half)):
+            remote(block_pair, block_pair, zs_sem.at[0], zr_sem.at[hd, half + d], peer(d, 0)).start()
+
+    pass_on(0)
+    stat_pair = statz.at[mirror]
+    remote(stat_pair, stat_pair, ss_sem.at[0], sr_sem.at[1], peer(half, 0)).wait_recv()
+    for d in reversed(range(1, half)):
+        remote(stat_pair, stat_pair, ss_sem.at[0], sr_sem.at[0], peer(d, 0)).start()
+    pass_on(1)
     row_send(0)
     all_but_one = statz.at[pl.ds(0, len(column))]
     stats = remote(all_but_one, all_but_one, ss_sem.at[0], sr_sem.at[0], peer(1, 0))
-    stats.wait_recv()
+    unmirrored = statz.at[pl.ds(0, len(column) - 2)]
+    remote(unmirrored, unmirrored, ss_sem.at[0], sr_sem.at[0], peer(1, 0)).wait_recv()
     column_sum = jnp.sum(statz[...], axis=0)
     staty_own[0] = column_sum
     staty[y] = column_sum
@@ -291,7 +311,11 @@
             for cc in range(2):
                 at = slice(zz * 16 + cc * 8, zz * 16 + cc * 8 + 8)
                 zsend[hd, zz * 2 + cc] = jnp.concatenate([sums[0][at], sums[1][at]], axis=0).astype(BF16)
-        zback[hd, z * 2 + core] = zsend[hd, z * 2 + core]
+        own_share = pltpu.make_async_copy(
+            zsend.at[hd, z * 2 + core], zback.at[hd, z * 2 + core], out_sem.at[5 + hd]
+        )
+        own_share.start()
+        outs.append(own_share)
         for d, e in column:
             remote(
                 zsend.at[hd, (z ^ d) * 2 + (core ^ e)], zback.at[hd, z * 2 + core], rzs_sem.at[0],
@@ -332,16 +356,6 @@
     for hd in range(2):
         landed = zback.at[hd, pl.ds(0, len(column))]
         remote(landed, landed, rzs_sem.at[0], rzr_sem.at[hd], peer(1, 0)).wait_recv()
-    for cc in range(2):
-        for hd in range(2):
-            total = zback[hd, cc].astype(F32)
-            for zz in range(1, NZ):
-                total = total + zback[hd, zz * 2 + cc].astype(F32)
-            cols = slice(cc * 256 + hd * HD, cc * 256 + (hd + 1) * HD)
-            gp_st[0, :, cols] = total[:8]
-            gp_st[1, :, cols] = total[8:]
-    outs.append(pltpu.make_async_copy(gp_st, gp_ref, out_sem.at[2]))
-    outs[-1].start()
 
     for copy in outs:
         copy.wait()
@@ -358,8 +372,8 @@
         remote(held, held, sem, sem, next_row).wait_send()
 
 
-def emit(gq_from, grkv_from, gp_from, gq_to, grkv_to, gp_to, sums, pairs, gq, grkv, fetch_sem, put_sem):
-    ways = [(gp_from, sums, None), (grkv_from, grkv, grkv_to)]
+def emit(gq_from, grkv_from, shares_from, gq_to, grkv_to, gp_to, shares, sums, pairs, gq, grkv, fetch_sem, put_sem):
+    ways = [(shares_from, shares, None), (grkv_from, grkv, grkv_to)]
     for i in range(4):
         at = pl.ds(i * 32, 32)
         ways.append((gq_from.at[at], gq.at[at], gq_to.at[at]))
@@ -367,6 +381,14 @@
     for fetch in fetches:
         fetch.start()
     fetches[0].wait()
+    for cc in range(2):
+        for hd in range(2):
+            total = shares[hd, cc].astype(F32)
+            for zz in range(1, NZ):
+                total = total + shares[hd, zz * 2 + cc].astype(F32)
+            cols = slice(cc * 256 + hd * HD, cc * 256 + (hd + 1) * HD)
+            sums[0, :, cols] = total[:8]
+            sums[1, :, cols] = total[8:]
     pairs[...] = jnp.stack([sums[0], sums[1]], axis=1).astype(BF16)
     puts = [pltpu.make_async_copy(pairs, gp_to, put_sem.at[0])]
     puts[0].start()
@@ -391,12 +413,11 @@
         out_shape=(
             jax.ShapeDtypeStruct(queries.shape, BF16),
             jax.ShapeDtypeStruct(roll_kv.shape, BF16),
-            jax.ShapeDtypeStruct((2, 8, 512), F32),
+            jax.ShapeDtypeStruct((2, ncol, 16, HD), BF16),
         ),
         in_specs=[hbm] * 6,
         out_specs=(hbm, hbm, hbm),
         scratch_shapes=[
-            vmem((2, 8, 512), F32),
             vmem(prefix_kv.shape, BF16),
             pltpu.SMEM((1,), jnp.int32),
             pltpu.SMEM((1,), jnp.int32),
@@ -424,19 +445,18 @@
             vmem((2, 2, NY - 1, near, HD), BF16),
             vmem((2, 2, near, HD), F32),
             vmem((2, ncol, 16, HD), BF16),
-            vmem((2, ncol, 16, HD), BF16),
             vmem((2, ROWS, 1024), BF16),
             vmem((2, 2, ROWS, 256), BF16),
             vmem((ROWS, 1024), BF16),
             vmem((2, ROWS, 256), BF16),
             sem((1,)), sem((2, NZ)),
-            sem((1,)), sem((1,)),
+            sem((1,)), sem((2,)),
             sem((1,)), sem((2, NY - 1)),
             sem((1,)), sem((1,)),
             sem((6,)), sem((3,)), sem((3,)),
             sem((1,)), sem((2,)),
             sem((1,)), sem((2,)),
-            sem((5,)), sem((2,)), sem((2,)),
+            sem((7,)), sem((2,)), sem((2,)),
         ],
         compiler_params=pltpu.CompilerParams(
             collective_id=0, has_side_effects=True, vmem_limit_bytes=60 * 2**20
@@ -453,7 +473,8 @@
         in_specs=[hbm] * 3,
         out_specs=[hbm] * 3,
         scratch_shapes=[
-            vmem((2, 8, 512), F32), vmem(prefix_kv.shape, BF16), vmem(queries.shape, BF16),
+            vmem((2, ncol, 16, HD), BF16), vmem((2, 8, 512), F32), vmem(prefix_kv.shape, BF16),
+            vmem(queries.shape, BF16),
             vmem(roll_kv.shape, BF16), sem((6,)), sem((6,)),
         ],
         compiler_params=pltpu.CompilerParams(vmem_limit_bytes=60 * 2**20),

time: 45.6 us -> 45.2 us (level)
  no operation moved by 1% of the time
where the time goes in v4:
time: 45.2 us; the launch traced here: 45 us
  Pallas kernels  43 us (95%)
  between operations  1.93 us (4%)
    pallas_call x1, Pallas kernels, local(): pl.pallas_call(kernel, out_shape=(jax.ShapeDtypeStruct(queries.shape, BF1...  41 us
    pallas_call x1, Pallas kernels, local(): pl.pallas_call(emit, out_shape=(jax.ShapeDtypeStruct(queries.shape, BF16)...  2 us

profile of v4, /device:TPU:1, one launch (start us, length us, event | category | flops | bytes accessed | tf_op | source)
XLA Modules:
  0.0 45.0 jit_solution(16307520588906151521)
XLA Ops:
  1.9 41.0 %prefix_attention_backward.1 = (bf16[128,2048]{1,0:T(8,128)(2,1)}, bf16[2,128,512]{2,1,0:T(8,128)(2,1)}, bf16[2,16,16,128]{3,2,1,0:T(8,128)(2,1)}) custom-call(bf16[128,2048]{1,0:T(8,128)(2,1)} %q_hbm.1, bf16[2,128,512]{2,1,0:T(8,128)(2,1)} %rkv_hbm.1, bf16[8,2,512]{2,1,0:T(2,128)(2,1)} %pkv_hbm.1, bf16[128,2048]{1,0:T(8,128)(2,1)} %do_hbm.1, ...), custom_call_target="tpu_custom_call" | custom-call | tf_op jit(solution)/shard_map/prefix_attention_backward/pallas_call | solution.py:411
  43.0 2.0 %emit.1 = (bf16[128,2048]{1,0:T(8,128)(2,1)}, bf16[2,128,512]{2,1,0:T(8,128)(2,1)}, bf16[8,2,512]{2,1,0:T(2,128)(2,1)}) custom-call(bf16[128,2048]{1,0:T(8,128)(2,1)} %get-tuple-element.6.gq_from, bf16[2,128,512]{2,1,0:T(8,128)(2,1)} %get-tuple-element.7.grkv_from, bf16[2,16,16,128]{3,2,1,0:T(8,128)(2,1)} %get-tuple-element.8.shares_from), custom_call_target="tpu_custom_call" | custom-call | tf_op jit(solution)/shard_map/emit/pallas_call | solution.py:466

commit v5 on v4

--- a/solution.py
+++ b/solution.py
@@ -131,8 +131,8 @@
     for copy in xcopies:
         copy.start()
 
-    def row_send(hd):
-        for d in range(NZ):
+    def row_send(hd, chips):
+        for d in chips:
             zz = z ^ d
             landed = zrecv.at[hd, pl.ds(zz * 2, 2)] if d else zrecv.at[hd, pl.ds(z * 2 + other, 1)]
             if d != half:
@@ -202,7 +202,9 @@
     for d in reversed(range(1, half)):
         remote(stat_pair, stat_pair, ss_sem.at[0], sr_sem.at[0], peer(d, 0)).start()
     pass_on(1)
-    row_send(0)
+    row_send(0, range(half))
+    row_send(1, range(half))
+    row_send(0, range(half, NZ))
     all_but_one = statz.at[pl.ds(0, len(column))]
     stats = remote(all_but_one, all_but_one, ss_sem.at[0], sr_sem.at[0], peer(1, 0))
     unmirrored = statz.at[pl.ds(0, len(column) - 2)]
@@ -215,7 +217,7 @@
             staty_own.at[0], staty.at[y], sys_sem.at[0], syr_sem.at[0], device((y + k) % NY, z, core)
         ).start()
 
-    row_send(1)
+    row_send(1, range(half, NZ))
     block(0, 0)
     block(1, 0)
 
@@ -380,6 +382,11 @@
     fetches = [pltpu.make_async_copy(way[0], way[1], fetch_sem.at[i]) for i, way in enumerate(ways)]
     for fetch in fetches:
         fetch.start()
+    puts = []
+    for i in range(1, len(ways)):
+        fetches[i].wait()
+        puts.append(pltpu.make_async_copy(ways[i][1], ways[i][2], put_sem.at[i]))
+        puts[-1].start()
     fetches[0].wait()
     for cc in range(2):
         for hd in range(2):
@@ -390,12 +397,8 @@
             sums[0, :, cols] = total[:8]
             sums[1, :, cols] = total[8:]
     pairs[...] = jnp.stack([sums[0], sums[1]], axis=1).astype(BF16)
-    puts = [pltpu.make_async_copy(pairs, gp_to, put_sem.at[0])]
-    puts[0].start()
-    for i in range(1, len(ways)):
-        fetches[i].wait()
-        puts.append(pltpu.make_async_copy(ways[i][1], ways[i][2], put_sem.at[i]))
-        puts[i].start()
+    puts.append(pltpu.make_async_copy(pairs, gp_to, put_sem.at[0]))
+    puts[-1].start()
     for put in puts:
         put.wait()
 

time: 45.2 us -> 44.5 us (0.985)
  Pallas kernels: 43 us -> 42.3 us
    pallas_call x1, Pallas kernels: 41 us -> 40.3 us  [local(): pl.pallas_call(kernel, out_shape=(jax.ShapeDtypeStruct(queries.shape, BF1...]
where the time goes in v5:
time: 44.5 us; the launch traced here: 44.3 us
  Pallas kernels  42.3 us (95%)
  between operations  1.93 us (4%)
    pallas_call x1, Pallas kernels, local(): pl.pallas_call(kernel, out_shape=(jax.ShapeDtypeStruct(queries.shape, BF1...  40.3 us
    pallas_call x1, Pallas kernels, local(): pl.pallas_call(emit, out_shape=(jax.ShapeDtypeStruct(queries.shape, BF16)...  2 us

profile of v5, /device:TPU:1, one launch (start us, length us, event | category | flops | bytes accessed | tf_op | source)
XLA Modules:
  0.0 44.3 jit_solution(16869266683973198447)
XLA Ops:
  1.9 40.3 %prefix_attention_backward.1 = (bf16[128,2048]{1,0:T(8,128)(2,1)}, bf16[2,128,512]{2,1,0:T(8,128)(2,1)}, bf16[2,16,16,128]{3,2,1,0:T(8,128)(2,1)}) custom-call(bf16[128,2048]{1,0:T(8,128)(2,1)} %q_hbm.1, bf16[2,128,512]{2,1,0:T(8,128)(2,1)} %rkv_hbm.1, bf16[8,2,512]{2,1,0:T(2,128)(2,1)} %pkv_hbm.1, bf16[128,2048]{1,0:T(8,128)(2,1)} %do_hbm.1, ...), custom_call_target="tpu_custom_call" | custom-call | tf_op jit(solution)/shard_map/prefix_attention_backward/pallas_call | solution.py:414
  42.3 2.0 %emit.1 = (bf16[128,2048]{1,0:T(8,128)(2,1)}, bf16[2,128,512]{2,1,0:T(8,128)(2,1)}, bf16[8,2,512]{2,1,0:T(2,128)(2,1)}) custom-call(bf16[128,2048]{1,0:T(8,128)(2,1)} %get-tuple-element.6.gq_from, bf16[2,128,512]{2,1,0:T(8,128)(2,1)} %get-tuple-element.7.grkv_from, bf16[2,16,16,128]{3,2,1,0:T(8,128)(2,1)} %get-tuple-element.8.shares_from), custom_call_target="tpu_custom_call" | custom-call | tf_op jit(solution)/shard_map/emit/pallas_call | solution.py:469

commit v6 on v5

--- a/solution.py
+++ b/solution.py
@@ -355,10 +355,6 @@
         back.start()
     outs = outs + backs
 
-    for hd in range(2):
-        landed = zback.at[hd, pl.ds(0, len(column))]
-        remote(landed, landed, rzs_sem.at[0], rzr_sem.at[hd], peer(1, 0)).wait_recv()
-
     for copy in outs:
         copy.wait()
     for copy in ocopies + xcopies:
@@ -372,6 +368,9 @@
         (zsend.at[:, pl.ds(0, len(column))], rzs_sem.at[0]),
     ):
         remote(held, held, sem, sem, next_row).wait_send()
+    for hd in range(2):
+        landed = zback.at[hd, pl.ds(0, len(column))]
+        remote(landed, landed, rzs_sem.at[0], rzr_sem.at[hd], peer(1, 0)).wait_recv()
 
 
 def emit(gq_from, grkv_from, shares_from, gq_to, grkv_to, gp_to, shares, sums, pairs, gq, grkv, fetch_sem, put_sem):

time: 44.5 us -> 44.4 us (level)
  no operation moved by 1% of the time
where the time goes in v6:
time: 44.4 us; the launch traced here: 44.2 us
  Pallas kernels  42.3 us (95%)
  between operations  1.93 us (4%)
    pallas_call x1, Pallas kernels, local(): pl.pallas_call(kernel, out_shape=(jax.ShapeDtypeStruct(queries.shape, BF1...  40.3 us
    pallas_call x1, Pallas kernels, local(): pl.pallas_call(emit, out_shape=(jax.ShapeDtypeStruct(queries.shape, BF16)...  2 us

profile of v6, /device:TPU:1, one launch (start us, length us, event | category | flops | bytes accessed | tf_op | source)
XLA Modules:
  0.0 44.2 jit_solution(2415755977696171286)
XLA Ops:
  1.9 40.3 %prefix_attention_backward.1 = (bf16[128,2048]{1,0:T(8,128)(2,1)}, bf16[2,128,512]{2,1,0:T(8,128)(2,1)}, bf16[2,16,16,128]{3,2,1,0:T(8,128)(2,1)}) custom-call(bf16[128,2048]{1,0:T(8,128)(2,1)} %q_hbm.1, bf16[2,128,512]{2,1,0:T(8,128)(2,1)} %rkv_hbm.1, bf16[8,2,512]{2,1,0:T(2,128)(2,1)} %pkv_hbm.1, bf16[128,2048]{1,0:T(8,128)(2,1)} %do_hbm.1, ...), custom_call_target="tpu_custom_call" | custom-call | tf_op jit(solution)/shard_map/prefix_attention_backward/pallas_call | solution.py:413
  42.2 2.0 %emit.1 = (bf16[128,2048]{1,0:T(8,128)(2,1)}, bf16[2,128,512]{2,1,0:T(8,128)(2,1)}, bf16[8,2,512]{2,1,0:T(2,128)(2,1)}) custom-call(bf16[128,2048]{1,0:T(8,128)(2,1)} %get-tuple-element.6.gq_from, bf16[2,128,512]{2,1,0:T(8,128)(2,1)} %get-tuple-element.7.grkv_from, bf16[2,16,16,128]{3,2,1,0:T(8,128)(2,1)} %get-tuple-element.8.shares_from), custom_call_target="tpu_custom_call" | custom-call | tf_op jit(solution)/shard_map/emit/pallas_call | solution.py:468
